TPU v7x, 32 devices: a whole 2x2x4 slice. The times are simulated.
32 devices in a mesh: blk: 8 (over z, x), group: 4 (over y, core).
Axes of the slice: x: 2, y: 2, z: 4, core: 2. Of those that a mesh axis runs over, the one named last changes fastest.
Arguments:
- image_embed: float32 [8192, 768], P(('blk', 'group')), may hold values from -6 to 6
- text_embed: float32 [8192, 768], P(('blk', 'group')), may hold values from -6 to 6
- image_lse: float32 [8192], P(('blk', 'group')), as said below
- text_lse: float32 [8192], P(('blk', 'group')), as said below
Outputs:
- grad_image: float32 [8192, 768], P(('blk', 'group'))
- grad_text: float32 [8192, 768], P(('blk', 'group'))
Inputs may be any that keep to these rules, and one draw needn't show every extreme that they name: `image_lse`: each value lies between c and c + 2, where c = 100 * sqrt(2 ln(1536) / 768). `text_lse`: each value lies between c and c + 2, where c = 100 * sqrt(2 ln(1536) / 768).
All inputs are finite; a program needn't handle non-finite values.
Results may differ from a plain program's by a relative error of at most 0.0003.
Values sent between devices are 32-bit elements; how exact they have to be, the bound alone decides.
A program may use at most 64 MiB of HBM per device.

v0:
```python
import jax
import jax.numpy as jnp
from jax import lax
from jax.sharding import PartitionSpec as P

STEPS = 3
PASSES = 2


logit_scale = 100.0
epsilon = 1e-06
highest = lax.Precision.HIGHEST


def shifted(block, axis, distance):
    devices = range(lax.axis_size(axis))
    route = [((i - distance) % len(devices), i) for i in devices]
    return lax.ppermute(block, axis, route)


def unit_rows(raw):
    inverse = lax.rsqrt(jnp.sum(raw * raw, axis=-1, keepdims=True) + epsilon)
    return (raw * inverse, inverse)


def project_back(grad_unit, unit, inverse):
    return (grad_unit - unit * jnp.sum(unit * grad_unit, axis=-1, keepdims=True)) * inverse


def per_device(image_embed, text_embed, image_lse, text_lse):
    image_unit, image_inverse = unit_rows(image_embed)
    text_unit, text_inverse = unit_rows(text_embed)
    row_count = image_embed.shape[0]
    identity = jnp.eye(row_count, dtype=jnp.float32)
    grad_image_unit = jnp.zeros_like(image_unit)
    grad_text_unit = jnp.zeros_like(text_unit)
    for pass_index in range(PASSES):
        if pass_index == 0:
            visiting = (text_unit, text_lse)
        else:
            visiting = shifted((text_unit, text_lse), "group", pass_index)
        carried = jnp.zeros_like(text_unit)
        for cycle_step in range(STEPS):
            if cycle_step > 0:
                visiting = shifted((visiting[0], visiting[1]), "blk", 1)
                carried = shifted(carried, "blk", 1)
            scores = logit_scale * lax.dot_general(
                image_unit, visiting[0], (((1,), (1,)), ((), ())), precision=highest
            )
            weight = 0.5 * (
                jnp.exp(scores - image_lse[:, None]) + jnp.exp(scores - visiting[1][None, :])
            )
            if cycle_step == 0 and pass_index == 0:
                weight = weight - identity
            grad_image_unit = grad_image_unit + logit_scale * jnp.dot(
                weight, visiting[0], precision=highest
            )
            tile_text = logit_scale * lax.dot_general(
                weight, image_unit, (((0,), (0,)), ((), ())), precision=highest
            )
            carried = carried + tile_text
        pass_total = shifted(carried, "blk", -(STEPS - 1))
        if pass_index > 0:
            pass_total = shifted(pass_total, "group", -pass_index)
        grad_text_unit = grad_text_unit + pass_total
    grad_image = project_back(grad_image_unit, image_unit, image_inverse)
    grad_text = project_back(grad_text_unit, text_unit, text_inverse)
    return (grad_image, grad_text)


def solution(mesh):
    return jax.shard_map(
        per_device,
        mesh=mesh,
        in_specs=(
            P(("blk", "group"), None),
            P(("blk", "group"), None),
            P(("blk", "group")),
            P(("blk", "group")),
        ),
        out_specs=(P(("blk", "group"), None), P(("blk", "group"), None)),
        check_vma=False,
    )
```

profile of v0, /device:TPU:0, one launch (start us, length us, event | category | flops | bytes accessed | tf_op | source)
XLA Modules:
  0.0 197.9 jit_solution(17652822297735506831)
XLA Ops:
  0.6 1.3 multiply_reduce_fusion.2
  2.0 0.1 broadcast_multiply_fusion
  2.1 0.5 collective-permute-start.4
  2.6 2.6 %collective-permute-start = (f32[256,768]{1,0:T(8,128)S(1)}, f32[256,768]{1,0:T(8,128)S(1)}, u32[]{:S(2)}, u32[]{:S(2)}) collective-permute-start(f32[256,768]{1,0:T(8,128)S(1)} %broadcast_multiply_fusion), channel_id=1, source_target_pairs={{28,0},{0,4},{4,8},{8,12},{12,16},{16,20},{20,24},{24,28},{29,1},{... | collective-permute-start | bytes 2359304 | tf_op jit(solution)/shard_map/ppermute | solution.py:18
  5.2 1.3 collective-permute-start.5
  6.5 1.5 collective-permute-start.1
  8.0 0.1 multiply_reduce_fusion.3
  8.2 0.7 copy-done.2
  8.9 0.9 convert_subtract_fusion
  9.8 1.0 convolution_multiply_fusion.5
  10.7 1.5 collective-permute-start.10
  12.3 2.0 %collective-permute-done.5 = f32[256]{0:T(256)S(1)} collective-permute-done((f32[256]{0:T(256)S(1)}, f32[256]{0:T(256)S(1)}, u32[]{:S(2)}, u32[]{:S(2)}) %collective-permute-start.5) | collective-permute-done | bytes 1056 | tf_op jit(solution)/shard_map/ppermute | solution.py:18
  14.3 2.3 %collective-permute-start.7 = (f32[256]{0:T(256)S(1)}, f32[256]{0:T(256)S(1)}, u32[]{:S(2)}, u32[]{:S(2)}) collective-permute-start(f32[256]{0:T(256)S(1)} %collective-permute-done.5), channel_id=1, source_target_pairs={{28,0},{0,4},{4,8},{8,12},{12,16},{16,20},{20,24},{24,28},{29,1},{... | collective-permute-start | bytes 3080 | tf_op jit(solution)/shard_map/ppermute | solution.py:18
  16.6 0.8 fusion.4
  17.4 8.4 %collective-permute-done.1 = f32[256]{0:T(256)S(1)} collective-permute-done((f32[256]{0:T(256)S(1)}, f32[256]{0:T(256)S(1)}, u32[]{:S(2)}, u32[]{:S(2)}) %collective-permute-start.1) | collective-permute-done | bytes 1056 | tf_op jit(solution)/shard_map/ppermute | solution.py:18
  25.8 16.9 %collective-permute-done.7 = f32[256]{0:T(256)S(1)} collective-permute-done((f32[256]{0:T(256)S(1)}, f32[256]{0:T(256)S(1)}, u32[]{:S(2)}, u32[]{:S(2)}) %collective-permute-start.7) | collective-permute-done | bytes 1056 | tf_op jit(solution)/shard_map/ppermute | solution.py:18
  42.7 0.9 add_multiply_fusion.2
  43.6 1.0 convolution_multiply_fusion.2
  44.6 1.8 collective-permute-start.13
  46.4 0.6 collective-permute-start.6
  47.0 0.9 add_multiply_fusion.4
  47.9 0.8 convolution_add_fusion.3
  48.8 2.5 %collective-permute-start.2 = (f32[256,768]{1,0:T(8,128)S(1)}, f32[256,768]{1,0:T(8,128)S(1)}, u32[]{:S(2)}, u32[]{:S(2)}) collective-permute-start(f32[256,768]{1,0:T(8,128)S(1)} %collective-permute-done), channel_id=1, source_target_pairs={{28,0},{0,4},{4,8},{8,12},{12,16},{16,20},{20,24},{24,28},{29,1},{... | collective-permute-start | bytes 2359304 | tf_op jit(solution)/shard_map/ppermute | solution.py:18
  51.3 1.0 fusion.1
  52.3 32.3 %collective-permute-done.6 = f32[256,768]{1,0:T(8,128)S(1)} collective-permute-done((f32[256,768]{1,0:T(8,128)S(1)}, f32[256,768]{1,0:T(8,128)S(1)}, u32[]{:S(2)}, u32[]{:S(2)}) %collective-permute-start.6) | collective-permute-done | bytes 786464 | tf_op jit(solution)/shard_map/ppermute | solution.py:18
  84.6 0.9 add_multiply_fusion.1
  85.5 1.0 fusion
  86.5 0.6 collective-permute-start.14
  87.1 0.8 fusion.5
  88.0 1.8 collective-permute-start.11
  89.8 28.5 %collective-permute-done.8 = f32[256,768]{1,0:T(8,128)S(1)} collective-permute-done((f32[256,768]{1,0:T(8,128)S(1)}, f32[256,768]{1,0:T(8,128)S(1)}, u32[]{:S(2)}, u32[]{:S(2)}) %collective-permute-start.8) | collective-permute-done | bytes 786464 | tf_op jit(solution)/shard_map/ppermute | solution.py:18
  118.3 0.9 add_multiply_fusion
  119.2 1.0 convolution_multiply_fusion
  120.2 15.0 %collective-permute-done.14 = f32[256,768]{1,0:T(8,128)S(1)} collective-permute-done((f32[256,768]{1,0:T(8,128)S(1)}, f32[256,768]{1,0:T(8,128)S(1)}, u32[]{:S(2)}, u32[]{:S(2)}) %collective-permute-start.14) | collective-permute-done | bytes 786464 | tf_op jit(solution)/shard_map/ppermute | solution.py:18
  135.3 1.1 collective-permute-start.15
  136.4 0.9 add_multiply_fusion.3
  137.3 0.9 convolution_multiply_fusion.3
  138.3 13.8 %collective-permute-done.11 = f32[256,768]{1,0:T(8,128)S(1)} collective-permute-done((f32[256,768]{1,0:T(8,128)S(1)}, f32[256,768]{1,0:T(8,128)S(1)}, u32[]{:S(2)}, u32[]{:S(2)}) %collective-permute-start.11) | collective-permute-done | bytes 786464 | tf_op jit(solution)/shard_map/ppermute | solution.py:18
  152.1 0.1 add.78
  152.2 33.9 %collective-permute-start.12 = (f32[256,768]{1,0:T(8,128)S(1)}, f32[256,768]{1,0:T(8,128)S(1)}, u32[]{:S(2)}, u32[]{:S(2)}) collective-permute-start(f32[256,768]{1,0:T(8,128)S(1)} %add.78), channel_id=1, source_target_pairs={{8,0},{12,4},{16,8},{20,12},{24,16},{28,20},{0,24},{4,28},{9,1},{1... | collective-permute-start | bytes 2359304 | tf_op jit(solution)/shard_map/ppermute | solution.py:18
  186.1 0.8 fusion.3
  187.1 0.8 convolution_add_fusion.1
  187.9 1.0 multiply_reduce_fusion.1
  188.9 1.1 subtract_multiply_fusion.1
  190.0 5.7 %collective-permute-done.12 = f32[256,768]{1,0:T(8,128)S(1)} collective-permute-done((f32[256,768]{1,0:T(8,128)S(1)}, f32[256,768]{1,0:T(8,128)S(1)}, u32[]{:S(2)}, u32[]{:S(2)}) %collective-permute-start.12) | collective-permute-done | bytes 786464 | tf_op jit(solution)/shard_map/ppermute | solution.py:18
  195.6 0.9 collective-permute-done.16
  196.6 0.2 multiply_reduce_fusion
  196.8 1.1 subtract_multiply_fusion
  (22 shorter events, 0.2 us)
Async XLA Ops:
  0.6 1.4 copy-start.1
  2.0 3.2 %copy-start.3 = (f32[256]{0:T(256)S(1)}, f32[256]{0:T(256)}, u32[]{:S(2)}) copy-start(f32[256]{0:T(256)} %param.7) | copy-start | bytes 3076
  2.0 6.0 %copy-start = (f32[256,768]{1,0:T(8,128)S(1)}, f32[256,768]{1,0:T(8,128)}, u32[]{:S(2)}) copy-start(f32[256,768]{1,0:T(8,128)} %param.4) | copy-start | bytes 2359300
  2.1 40.6 %collective-permute-start.4 = (f32[256,768]{1,0:T(8,128)S(1)}, f32[256,768]{1,0:T(8,128)S(1)}, u32[]{:S(2)}, u32[]{:S(2)}) collective-permute-start(f32[256,768]{1,0:T(8,128)S(1)} %broadcast_multiply_fusion), channel_id=1, source_target_pairs={{3,0},{0,1},{1,2},{2,3},{7,4},{4,5},{5,6},{6,7},{11,8},{8,9},{9,10... | collective-permute-start | bytes 2359304 | tf_op jit(solution)/shard_map/ppermute | solution.py:18
  2.6 43.8 %collective-permute-start = (f32[256,768]{1,0:T(8,128)S(1)}, f32[256,768]{1,0:T(8,128)S(1)}, u32[]{:S(2)}, u32[]{:S(2)}) collective-permute-start(f32[256,768]{1,0:T(8,128)S(1)} %broadcast_multiply_fusion), channel_id=1, source_target_pairs={{28,0},{0,4},{4,8},{8,12},{12,16},{16,20},{20,24},{24,28},{29,1},{... | collective-permute-start | bytes 2359304 | tf_op jit(solution)/shard_map/ppermute | solution.py:18
  5.2 9.1 %collective-permute-start.5 = (f32[256]{0:T(256)S(1)}, f32[256]{0:T(256)S(1)}, u32[]{:S(2)}, u32[]{:S(2)}) collective-permute-start(f32[256]{0:T(256)S(1)} %copy-done.3), channel_id=1, source_target_pairs={{3,0},{0,1},{1,2},{2,3},{7,4},{4,5},{5,6},{6,7},{11,8},{8,9},{9,10... | collective-permute-start | bytes 3080 | tf_op jit(solution)/shard_map/ppermute | solution.py:18
  6.5 19.3 %collective-permute-start.1 = (f32[256]{0:T(256)S(1)}, f32[256]{0:T(256)S(1)}, u32[]{:S(2)}, u32[]{:S(2)}) collective-permute-start(f32[256]{0:T(256)S(1)} %copy-done.3), channel_id=1, source_target_pairs={{28,0},{0,4},{4,8},{8,12},{12,16},{16,20},{20,24},{24,28},{29,1},{... | collective-permute-start | bytes 3080 | tf_op jit(solution)/shard_map/ppermute | solution.py:18
  8.2 0.7 copy-start.2
  10.7 38.0 %collective-permute-start.10 = (f32[256,768]{1,0:T(8,128)S(1)}, f32[256,768]{1,0:T(8,128)S(1)}, u32[]{:S(2)}, u32[]{:S(2)}) collective-permute-start(f32[256,768]{1,0:T(8,128)S(1)} %convolution_multiply_fusion.5), channel_id=1, source_target_pairs={{28,0},{0,4},{4,8},{8,12},{12,16},{16,20},{20,24},{24,28},{29,1},{... | collective-permute-start | bytes 2359304 | tf_op jit(solution)/shard_map/ppermute | solution.py:18
  14.3 28.4 %collective-permute-start.7 = (f32[256]{0:T(256)S(1)}, f32[256]{0:T(256)S(1)}, u32[]{:S(2)}, u32[]{:S(2)}) collective-permute-start(f32[256]{0:T(256)S(1)} %collective-permute-done.5), channel_id=1, source_target_pairs={{28,0},{0,4},{4,8},{8,12},{12,16},{16,20},{20,24},{24,28},{29,1},{... | collective-permute-start | bytes 3080 | tf_op jit(solution)/shard_map/ppermute | solution.py:18
  25.8 110.6 %collective-permute-start.3 = (f32[256]{0:T(256)S(1)}, f32[256]{0:T(256)S(1)}, u32[]{:S(2)}, u32[]{:S(2)}) collective-permute-start(f32[256]{0:T(256)S(1)} %collective-permute-done.1), channel_id=1, source_target_pairs={{28,0},{0,4},{4,8},{8,12},{12,16},{16,20},{20,24},{24,28},{29,1},{... | collective-permute-start | bytes 3080 | tf_op jit(solution)/shard_map/ppermute | solution.py:18
  42.7 45.3 %collective-permute-start.9 = (f32[256]{0:T(256)S(1)}, f32[256]{0:T(256)S(1)}, u32[]{:S(2)}, u32[]{:S(2)}) collective-permute-start(f32[256]{0:T(256)S(1)} %collective-permute-done.7), channel_id=1, source_target_pairs={{28,0},{0,4},{4,8},{8,12},{12,16},{16,20},{20,24},{24,28},{29,1},{... | collective-permute-start | bytes 3080 | tf_op jit(solution)/shard_map/ppermute | solution.py:18
  44.6 40.9 %collective-permute-start.13 = (f32[256,768]{1,0:T(8,128)S(1)}, f32[256,768]{1,0:T(8,128)S(1)}, u32[]{:S(2)}, u32[]{:S(2)}) collective-permute-start(f32[256,768]{1,0:T(8,128)S(1)} %convolution_multiply_fusion.2), channel_id=1, source_target_pairs={{28,0},{0,4},{4,8},{8,12},{12,16},{16,20},{20,24},{24,28},{29,1},{... | collective-permute-start | bytes 2359304 | tf_op jit(solution)/shard_map/ppermute | solution.py:18
  46.4 38.2 %collective-permute-start.6 = (f32[256,768]{1,0:T(8,128)S(1)}, f32[256,768]{1,0:T(8,128)S(1)}, u32[]{:S(2)}, u32[]{:S(2)}) collective-permute-start(f32[256,768]{1,0:T(8,128)S(1)} %collective-permute-done.4), channel_id=1, source_target_pairs={{28,0},{0,4},{4,8},{8,12},{12,16},{16,20},{20,24},{24,28},{29,1},{... | collective-permute-start | bytes 2359304 | tf_op jit(solution)/shard_map/ppermute | solution.py:18
  48.8 87.7 %collective-permute-start.2 = (f32[256,768]{1,0:T(8,128)S(1)}, f32[256,768]{1,0:T(8,128)S(1)}, u32[]{:S(2)}, u32[]{:S(2)}) collective-permute-start(f32[256,768]{1,0:T(8,128)S(1)} %collective-permute-done), channel_id=1, source_target_pairs={{28,0},{0,4},{4,8},{8,12},{12,16},{16,20},{20,24},{24,28},{29,1},{... | collective-permute-start | bytes 2359304 | tf_op jit(solution)/shard_map/ppermute | solution.py:18
  84.6 33.7 %collective-permute-start.8 = (f32[256,768]{1,0:T(8,128)S(1)}, f32[256,768]{1,0:T(8,128)S(1)}, u32[]{:S(2)}, u32[]{:S(2)}) collective-permute-start(f32[256,768]{1,0:T(8,128)S(1)} %collective-permute-done.6), channel_id=1, source_target_pairs={{28,0},{0,4},{4,8},{8,12},{12,16},{16,20},{20,24},{24,28},{29,1},{... | collective-permute-start | bytes 2359304 | tf_op jit(solution)/shard_map/ppermute | solution.py:18
  86.5 48.7 %collective-permute-start.14 = (f32[256,768]{1,0:T(8,128)S(1)}, f32[256,768]{1,0:T(8,128)S(1)}, u32[]{:S(2)}, u32[]{:S(2)}) collective-permute-start(f32[256,768]{1,0:T(8,128)S(1)} %fusion), channel_id=1, source_target_pairs={{28,0},{0,4},{4,8},{8,12},{12,16},{16,20},{20,24},{24,28},{29,1},{... | collective-permute-start | bytes 2359304 | tf_op jit(solution)/shard_map/ppermute | solution.py:18
  88.0 64.1 %collective-permute-start.11 = (f32[256,768]{1,0:T(8,128)S(1)}, f32[256,768]{1,0:T(8,128)S(1)}, u32[]{:S(2)}, u32[]{:S(2)}) collective-permute-start(f32[256,768]{1,0:T(8,128)S(1)} %fusion.1), channel_id=1, source_target_pairs={{28,0},{0,4},{4,8},{8,12},{12,16},{16,20},{20,24},{24,28},{29,1},{... | collective-permute-start | bytes 2359304 | tf_op jit(solution)/shard_map/ppermute | solution.py:18
  135.3 51.6 %collective-permute-start.15 = (f32[256,768]{1,0:T(8,128)S(1)}, f32[256,768]{1,0:T(8,128)S(1)}, u32[]{:S(2)}, u32[]{:S(2)}) collective-permute-start(f32[256,768]{1,0:T(8,128)S(1)} %add.80), channel_id=1, source_target_pairs={{8,0},{12,4},{16,8},{20,12},{24,16},{28,20},{0,24},{4,28},{9,1},{1... | collective-permute-start | bytes 2359304 | tf_op jit(solution)/shard_map/ppermute | solution.py:18
  152.2 43.4 %collective-permute-start.12 = (f32[256,768]{1,0:T(8,128)S(1)}, f32[256,768]{1,0:T(8,128)S(1)}, u32[]{:S(2)}, u32[]{:S(2)}) collective-permute-start(f32[256,768]{1,0:T(8,128)S(1)} %add.78), channel_id=1, source_target_pairs={{8,0},{12,4},{16,8},{20,12},{24,16},{28,20},{0,24},{4,28},{9,1},{1... | collective-permute-start | bytes 2359304 | tf_op jit(solution)/shard_map/ppermute | solution.py:18
  187.0 9.6 %collective-permute-start.16 = (f32[256,768]{1,0:T(8,128)S(1)}, f32[256,768]{1,0:T(8,128)S(1)}, u32[]{:S(2)}, u32[]{:S(2)}) collective-permute-start(f32[256,768]{1,0:T(8,128)S(1)} %collective-permute-done.15), channel_id=1, source_target_pairs={{1,0},{2,1},{3,2},{0,3},{5,4},{6,5},{7,6},{4,7},{9,8},{10,9},{11,1... | collective-permute-start | bytes 2359304 | tf_op jit(solution)/shard_map/ppermute | solution.py:18
where the time goes:
time: 199 us; the launch traced here: 198 us
  waiting for transfers between devices  124 us (62%)
  starting transfers between devices  52.2 us (26%)
  matrix products  16.4 us (8%)
  other arithmetic  4.18 us (2%)
    ppermute x17, waiting for transfers between devices, shifted(): return lax.ppermute(block, axis, route)  124 us
    ppermute x17, starting transfers between devices, shifted(): return lax.ppermute(block, axis, route)  52.2 us
    dot_general x6, matrix products, per_device(): lax.dot_general(weight, image_unit, (((0,), (0,)), ((), ())), precision=h...  5.85 us
    dot_general x6, matrix products, per_device(): lax.dot_general(image_unit, visiting[0], (((1,), (1,)), ((), ())), precis...  5.36 us
    dot_general x6, matrix products, per_device(): jnp.dot(weight, visiting[0], precision=highest)  5.16 us
  transfers between devices with their start and end apart: 17, of which 9 were waited for; matrix products, arithmetic and copies ran while one was open for 9% of the time, Pallas kernels for 0%

commit v1 on v0

v1 whole, which is shorter than its diff:
```python
import functools

import jax
import jax.numpy as jnp
from jax import lax
from jax.experimental import pallas as pl
from jax.experimental.pallas import tpu as pltpu
from jax.sharding import PartitionSpec as P

MESH = pl.DeviceIdType.MESH
CHUNKS = 4
OWN, MID, FAR = 0, 1, 2
TO_FAR, TO_MID, TO_IMAGE, BACK_FAR, BACK_MID, BACK_IMAGE = range(6)

logit_scale = 100.0
epsilon = 1e-06
NT = (((1,), (1,)), ((), ()))
NN = (((1,), (0,)), ((), ()))


def split(value):
    high = value.astype(jnp.bfloat16)
    return high, (value - high.astype(jnp.float32)).astype(jnp.bfloat16)


def dot_split(a, b, dims):
    dot = functools.partial(lax.dot_general, dimension_numbers=dims, preferred_element_type=jnp.float32)
    return dot(a[0], b[0]) + (dot(a[0], b[1]) + dot(a[1], b[0]))


def unit_rows(raw):
    inverse = lax.rsqrt(jnp.sum(raw * raw, axis=-1, keepdims=True) + epsilon)
    return raw * inverse, inverse


def project_back(grad_unit, raw):
    unit, inverse = unit_rows(raw)
    return (grad_unit - unit * jnp.sum(unit * grad_unit, axis=-1, keepdims=True)) * inverse


def kernel(
    n_blk, n_group,
    image_ref, text_ref, image_lse_ref, text_lse_ref, grad_image_ref, grad_text_ref,
    raw_far, raw_mid, raw_image, lse_far, lse_mid, lse_image,
    text_high, text_low, text_column, image_high, image_low, weights,
    g_own, g_far, g_mid, got_far, got_mid, g_image, got_image,
    send_sem, recv_sem,
):
    rows, width = image_ref.shape
    chunk = rows // CHUNKS
    blk, group = lax.axis_index("blk"), lax.axis_index("group")
    odd = lax.rem(blk, 2) == 1
    even = lax.rem(blk, 2) == 0
    ahead = (lax.rem(blk + 2, n_blk), group)
    behind = (lax.rem(blk + n_blk - 2, n_blk), group)
    partner = (blk + 1 - 2 * lax.rem(blk, 2), group)
    higher = (blk, lax.rem(group + 1, n_group))
    lower = (blk, lax.rem(group + n_group - 1, n_group))

    barrier = pltpu.get_barrier_semaphore()
    for device in (ahead, behind, partner, higher, lower):
        pl.semaphore_signal(barrier, inc=1, device_id=device, device_id_type=MESH)
    pl.semaphore_wait(barrier, 5)

    def part(k):
        return pl.ds(pl.multiple_of(k * chunk, chunk), chunk)

    def copy(src, dst, kind, slot, device):
        return pltpu.make_async_remote_copy(
            src_ref=src, dst_ref=dst, send_sem=send_sem.at[kind, slot], recv_sem=recv_sem.at[kind, slot],
            device_id=device, device_id_type=MESH,
        )

    def to_far(k):
        return copy(text_ref.at[part(k)], raw_far.at[part(k)], TO_FAR, k, ahead)

    def to_mid(k, source):
        return copy(source.at[part(k)], raw_mid.at[part(k)], TO_MID, k, partner)

    def lse_to_far():
        return copy(text_lse_ref, lse_far, TO_FAR, CHUNKS, ahead)

    def lse_to_mid(source):
        return copy(source, lse_mid, TO_MID, CHUNKS, partner)

    def to_image():
        return copy(image_ref, raw_image, TO_IMAGE, 0, lower)

    def lse_to_image():
        return copy(image_lse_ref, lse_image, TO_IMAGE, CHUNKS, lower)

    def back_far(k):
        return copy(g_far.at[part(k)], got_far.at[part(k)], BACK_FAR, k, behind)

    def back_mid(k):
        return copy(g_mid.at[part(k)], got_mid.at[part(k)], BACK_MID, k, partner)

    def back_image():
        return copy(g_image.at[pl.ds(rows, rows)], got_image, BACK_IMAGE, 0, higher)

    lse_to_far().start()
    lse_to_image().start()

    @pl.when(even)
    def _():
        lse_to_mid(text_lse_ref).start()

    for k in range(CHUNKS):
        to_far(k).start()

        @pl.when(even)
        def _():
            to_mid(k, text_ref).start()

        if k == 0:
            to_image().start()

    def take_text(which, raw, k):
        unit, _ = unit_rows(raw[part(k), :])
        text_high[which, part(k), :], text_low[which, part(k), :] = split(unit)

    def take_column(which, lse):
        text_column[which] = jnp.transpose(jnp.broadcast_to(lse[...], (128, rows)))

    def take_image(first, raw):
        @pl.loop(0, CHUNKS)
        def _(k):
            unit, _ = unit_rows(raw[part(k), :])
            here = pl.ds(pl.multiple_of(first + k * chunk, chunk), chunk)
            image_high[here, :], image_low[here, :] = split(unit)

    def tile(which, k, columns, lse, diagonal=False):
        text = (text_high[which, part(k), :], text_low[which, part(k), :])
        image = (image_high[columns, :], image_low[columns, :])
        scores = logit_scale * dot_split(text, image, NT)
        weight = (0.5 * logit_scale) * (
            jnp.exp(scores - lse) + jnp.exp(scores - text_column[which, part(k), 0:1])
        )
        if diagonal:
            row = lax.broadcasted_iota(jnp.int32, weight.shape, 0) + k * chunk
            column = lax.broadcasted_iota(jnp.int32, weight.shape, 1)
            weight = weight - jnp.where(row == column, logit_scale, 0.0)
        weights[which, part(k), columns] = weight
        return dot_split(split(weight), image, NN)

    first, second, both = pl.ds(0, rows), pl.ds(rows, rows), pl.ds(0, 2 * rows)

    def image_grad(which, half):
        weight = split(jnp.transpose(weights[which, :, half]))
        return dot_split(weight, (text_high[which], text_low[which]), NN)

    take_column(OWN, text_lse_ref)
    take_image(0, image_ref)

    @pl.loop(0, CHUNKS)
    def _(k):
        take_text(OWN, text_ref, k)
        g_own[part(k), :] = tile(OWN, k, first, image_lse_ref[...], diagonal=True)

    lse_to_far().wait_recv()

    @pl.when(odd)
    def _():
        lse_to_mid(lse_far).start()

    take_column(FAR, lse_far)

    def receive_far(k):
        to_far(k).wait_recv()

        @pl.when(odd)
        def _():
            to_mid(k, raw_far).start()

    receive_far(0)
    receive_far(1)
    lse_to_image().wait_recv()
    to_image().wait_recv()
    take_image(rows, raw_image)

    @pl.loop(0, CHUNKS)
    def _(k):
        g_own[part(k), :] += tile(OWN, k, second, lse_image[...])

    lse_to_mid(text_lse_ref).wait_recv()
    take_column(MID, lse_mid)
    both_lse = jnp.concatenate([image_lse_ref[...], lse_image[...]], axis=1)

    def pass_on(k):
        back_mid(k).wait_recv()
        g_far[part(k), :] += got_mid[part(k), :]
        back_far(k).start()

    @pl.loop(0, CHUNKS + 1)
    def _(k):
        @pl.when(k < CHUNKS)
        def _():
            take_text(FAR, raw_far, k)
            g_far[part(k), :] = tile(FAR, k, both, both_lse)

            @pl.when(even)
            def _():
                back_far(k).start()

        @pl.when(k + 2 < CHUNKS)
        def _():
            receive_far(k + 2)

        @pl.when(k > 0)
        def _():
            to_mid(k - 1, text_ref).wait_recv()
            take_text(MID, raw_mid, k - 1)
            g_mid[part(k - 1), :] = tile(MID, k - 1, both, both_lse)
            back_mid(k - 1).start()

        @pl.when(jnp.logical_and(odd, k > 1))
        def _():
            pass_on(k - 2)

    g_image[second, :] = image_grad(OWN, second) + image_grad(MID, second) + image_grad(FAR, second)
    back_image().start()

    @pl.when(odd)
    def _():
        pass_on(CHUNKS - 1)

    g_image[first, :] = image_grad(OWN, first) + image_grad(MID, first) + image_grad(FAR, first)
    back_image().wait_recv()

    @pl.loop(0, CHUNKS)
    def _(k):
        grad_image_ref[part(k), :] = project_back(
            g_image[part(k), :] + got_image[part(k), :], image_ref[part(k), :]
        )

    @pl.loop(0, CHUNKS)
    def _(k):
        @pl.when(even)
        def _():
            back_mid(k).wait_recv()
            g_own[part(k), :] += got_mid[part(k), :]

        back_far(k).wait_recv()
        grad_text_ref[part(k), :] = project_back(
            g_own[part(k), :] + got_far[part(k), :], text_ref[part(k), :]
        )

    lse_to_far().wait_send()
    lse_to_mid(text_lse_ref).wait_send()
    lse_to_image().wait_send()
    to_image().wait_send()
    back_image().wait_send()

    @pl.loop(0, CHUNKS)
    def _(k):
        to_far(k).wait_send()
        to_mid(k, text_ref).wait_send()
        back_far(k).wait_send()
        back_mid(k).wait_send()


def solution(mesh):
    n_blk, n_group = mesh.shape["blk"], mesh.shape["group"]

    def per_device(image_embed, text_embed, image_lse, text_lse):
        rows, width = image_embed.shape
        block = jax.ShapeDtypeStruct((rows, width), jnp.float32)
        whole = pltpu.VMEM((rows, width), jnp.float32)
        line = pltpu.VMEM((1, rows), jnp.float32)
        return pl.pallas_call(
            functools.partial(kernel, n_blk, n_group),
            out_shape=(block, block),
            in_specs=[pl.BlockSpec(memory_space=pltpu.VMEM)] * 4,
            out_specs=[pl.BlockSpec(memory_space=pltpu.VMEM)] * 2,
            scratch_shapes=[
                whole, whole, whole, line, line, line,
                pltpu.VMEM((3, rows, width), jnp.bfloat16),
                pltpu.VMEM((3, rows, width), jnp.bfloat16),
                pltpu.VMEM((3, rows, 128), jnp.float32),
                pltpu.VMEM((2 * rows, width), jnp.bfloat16),
                pltpu.VMEM((2 * rows, width), jnp.bfloat16),
                pltpu.VMEM((3, rows, 2 * rows), jnp.float32),
                whole, whole, whole, whole, whole,
                pltpu.VMEM((2 * rows, width), jnp.float32),
                whole,
                pltpu.SemaphoreType.DMA((6, CHUNKS + 1)),
                pltpu.SemaphoreType.DMA((6, CHUNKS + 1)),
            ],
            compiler_params=pltpu.CompilerParams(
                collective_id=0, has_side_effects=True, vmem_limit_bytes=40 * 1024 * 1024
            ),
        )(image_embed, text_embed, image_lse.reshape(1, rows), text_lse.reshape(1, rows))

    spec = P(("blk", "group"), None)
    line = P(("blk", "group"))
    return jax.shard_map(
        per_device, mesh=mesh, in_specs=(spec, spec, line, line), out_specs=(spec, spec), check_vma=False
    )
```

time: 199 us -> 57.4 us (0.29)
  waiting for transfers between devices: 124 us -> 0 us
  starting transfers between devices: 52.2 us -> 0 us
  Pallas kernels: 0 us -> 51.3 us
  matrix products: 16.4 us -> 0 us
  other arithmetic: 4.18 us -> 0 us
  local copies, waits for them, and re-layouts: 0.69 us -> 4.71 us
    ppermute x17 -> x0, waiting for transfers between devices: 124 us -> none  [shifted(): return lax.ppermute(block, axis, route)]
    ppermute x17 -> x0, starting transfers between devices: 52.2 us -> none  [shifted(): return lax.ppermute(block, axis, route)]
    pallas_call x0 -> x1, Pallas kernels: none -> 51.3 us  [per_device(): pl.pallas_call(functools.partial(kernel, n_blk, n_group), out_shape=(bloc...]
    dot_general x18 -> x0, matrix products: 16.4 us -> none  [the longest x6 5.85 us: per_device(): lax.dot_general(weight, image_unit, (((0,), (0,)), ((), ())), precision=h...]
    unnamed x8 -> x10, local copies, waits for them, and re-layouts: 0.69 us -> 4.71 us
    mul x3 -> x0, other arithmetic: 2.25 us -> none  [the longest x2 2.13 us: project_back(): (grad_unit - unit * jnp.sum(unit * grad_unit, axis=-1, keepdims=True)) *...]
  transfers between devices with their start and end apart: 17 -> 0, of which waited for: 9 -> 0; matrix products, arithmetic and copies ran while one was open for 9% -> 0% of each run, Pallas kernels for 0% -> 0%
where the time goes in v1:
time: 57.4 us; the launch traced here: 56.7 us
  Pallas kernels  51.3 us (89%)
  local copies, waits for them, and re-layouts  4.71 us (8%)
  between operations  0.66 us (1%)
    pallas_call x1, Pallas kernels, per_device(): pl.pallas_call(functools.partial(kernel, n_blk, n_group), out_shape=(bloc...  51.3 us
    unnamed x10, local copies, waits for them, and re-layouts  4.71 us

profile of v1, /device:TPU:0, one launch (start us, length us, event | category | flops | bytes accessed | tf_op | source)
XLA Modules:
  0.0 56.7 jit_solution(9256647009538796766)
XLA Ops:
  0.6 0.0 copy-start.3
  0.6 0.0 copy-start.2
  0.7 0.7 %copy-done.3 = f32[256]{0:T(256)S(1)} copy-done((f32[256]{0:T(256)S(1)}, f32[256]{0:T(256)}, u32[]{:S(2)}) %copy-start.3) | copy-done | bytes 1048
  1.3 0.0 copy-done.2
  1.3 0.0 copy-start
  1.3 1.1 %copy-done = f32[256,768]{1,0:T(8,128)S(1)} copy-done((f32[256,768]{1,0:T(8,128)S(1)}, f32[256,768]{1,0:T(8,128)}, u32[]{:S(2)}) %copy-start) | copy-done | bytes 786456
  2.5 0.0 copy-start.1
  2.5 1.1 %copy-done.1 = f32[256,768]{1,0:T(8,128)S(1)} copy-done((f32[256,768]{1,0:T(8,128)S(1)}, f32[256,768]{1,0:T(8,128)}, u32[]{:S(2)}) %copy-start.1) | copy-done | bytes 786456
  3.6 51.3 %shard_map.59 = (f32[256,768]{1,0:T(8,128)S(1)}, f32[256,768]{1,0:T(8,128)S(1)}) custom-call(f32[256,768]{1,0:T(8,128)S(1)} %copy-done, f32[256,768]{1,0:T(8,128)S(1)} %copy-done.1, f32[1,256]{1,0:T(1,128)S(1)} %bitcast.2, f32[1,256]{1,0:T(1,128)S(1)} %bitcast.3), custom_call_target="tpu_custom_call" | custom-call | tf_op jit(solution)/shard_map/pallas_call | solution.py:270
  54.9 0.9 %copy.8 = f32[256,768]{1,0:T(8,128)} copy(f32[256,768]{1,0:T(8,128)S(1)} %get-tuple-element.4) | data formatting | bytes 1572864
  55.8 0.9 %copy.9 = f32[256,768]{1,0:T(8,128)} copy(f32[256,768]{1,0:T(8,128)S(1)} %get-tuple-element.5) | data formatting | bytes 1572864
Async XLA Ops:
  0.6 0.7 %copy-start.3 = (f32[256]{0:T(256)S(1)}, f32[256]{0:T(256)}, u32[]{:S(2)}) copy-start(f32[256]{0:T(256)} %param.7) | copy-start | bytes 3076
  0.6 0.7 %copy-start.2 = (f32[256]{0:T(256)S(1)}, f32[256]{0:T(256)}, u32[]{:S(2)}) copy-start(f32[256]{0:T(256)} %param.6) | copy-start | bytes 3076
  1.3 1.1 %copy-start = (f32[256,768]{1,0:T(8,128)S(1)}, f32[256,768]{1,0:T(8,128)}, u32[]{:S(2)}) copy-start(f32[256,768]{1,0:T(8,128)} %image_ref.1) | copy-start | bytes 2359300
  2.5 1.1 %copy-start.1 = (f32[256,768]{1,0:T(8,128)S(1)}, f32[256,768]{1,0:T(8,128)}, u32[]{:S(2)}) copy-start(f32[256,768]{1,0:T(8,128)} %text_ref.1) | copy-start | bytes 2359300

commit v2 on v1

v2 whole, which is shorter than its diff:
```python
import functools

import jax
import jax.numpy as jnp
from jax import lax
from jax.experimental import pallas as pl
from jax.experimental.pallas import tpu as pltpu
from jax.sharding import PartitionSpec as P

MESH = pl.DeviceIdType.MESH
CHUNKS = 4
PIECES = 8
DIRECT = 0
OWN, MID, FAR = 0, 1, 2
TO_FAR, TO_MID, TO_IMAGE, BACK_FAR, BACK_MID, BACK_IMAGE = range(6)

logit_scale = 100.0
epsilon = 1e-06
NT = (((1,), (1,)), ((), ()))
NN = (((1,), (0,)), ((), ()))


def split(value):
    high = value.astype(jnp.bfloat16)
    return high, (value - high.astype(jnp.float32)).astype(jnp.bfloat16)


def dot_split(a, b, dims):
    dot = functools.partial(lax.dot_general, dimension_numbers=dims, preferred_element_type=jnp.float32)
    rows = a[0].shape[0]
    by_high = dot(jnp.concatenate(a, axis=0), b[0])
    return by_high[:rows] + (by_high[rows:] + dot(a[0], b[1]))


def unit_rows(raw):
    inverse = lax.rsqrt(jnp.sum(raw * raw, axis=-1, keepdims=True) + epsilon)
    return raw * inverse, inverse


def project_back(grad_unit, raw):
    unit, inverse = unit_rows(raw)
    return (grad_unit - unit * jnp.sum(unit * grad_unit, axis=-1, keepdims=True)) * inverse


def kernel(
    n_blk, n_group,
    image_hbm, text_hbm, image_lse_hbm, text_lse_hbm, grad_image_hbm, grad_text_hbm,
    image_ref, text_ref, image_lse_ref, text_lse_ref, load_sem,
    grad_image_ref, grad_text_ref, store_sem,
    raw_far, raw_mid, raw_image, lse_far, lse_mid, lse_image,
    text_high, text_low, text_column, image_high, image_low, weights,
    g_own, g_far, g_mid, got_far, got_mid, g_image, got_image,
    send_sem, recv_sem,
):
    rows, width = image_ref.shape
    chunk = rows // CHUNKS
    blk, group = lax.axis_index("blk"), lax.axis_index("group")
    odd = lax.rem(blk, 2) == 1
    even = lax.rem(blk, 2) == 0
    ahead = (lax.rem(blk + 2, n_blk), group)
    behind = (lax.rem(blk + n_blk - 2, n_blk), group)
    partner = (blk + 1 - 2 * lax.rem(blk, 2), group)
    onward = (lax.rem(blk + 1, n_blk), group)
    diagonal = (lax.rem(blk + n_blk - 1 + 2 * lax.rem(blk, 2), n_blk), group)
    higher = (blk, lax.rem(group + 1, n_group))
    lower = (blk, lax.rem(group + n_group - 1, n_group))

    load_text = pltpu.make_async_copy(text_hbm, text_ref, load_sem.at[0])
    load_image = pltpu.make_async_copy(image_hbm, image_ref, load_sem.at[1])
    load_text_lse = pltpu.make_async_copy(text_lse_hbm, text_lse_ref, load_sem.at[2])
    load_image_lse = pltpu.make_async_copy(image_lse_hbm, image_lse_ref, load_sem.at[3])
    for load in (load_image, load_text, load_text_lse, load_image_lse):
        load.start()

    barrier = pltpu.get_barrier_semaphore()
    for device in (ahead, behind, partner, diagonal, higher, lower):
        pl.semaphore_signal(barrier, inc=1, device_id=device, device_id_type=MESH)
    pl.semaphore_wait(barrier, 6)

    def part(k):
        return pl.ds(pl.multiple_of(k * chunk, chunk), chunk)

    def piece(j):
        size = rows // PIECES
        return pl.ds(pl.multiple_of(j * size, size), size)

    def copy(src, dst, kind, slot, device):
        return pltpu.make_async_remote_copy(
            src_ref=src, dst_ref=dst, send_sem=send_sem.at[kind, slot], recv_sem=recv_sem.at[kind, slot],
            device_id=device, device_id_type=MESH,
        )

    def to_far(k):
        return copy(text_hbm.at[piece(k)], raw_far.at[piece(k)], TO_FAR, k, ahead)

    def to_mid(k, source):
        return copy(source.at[piece(k)], raw_mid.at[piece(k)], TO_MID, k, partner)

    def store_image(k):
        return pltpu.make_async_copy(grad_image_ref.at[part(k)], grad_image_hbm.at[part(k)], store_sem.at[0, k])

    def store_text(k):
        return pltpu.make_async_copy(grad_text_ref.at[part(k)], grad_text_hbm.at[part(k)], store_sem.at[1, k])

    def lse_to_far():
        return copy(text_lse_hbm, lse_far, TO_FAR, PIECES, ahead)

    def to_mid_direct(j):
        return copy(text_hbm.at[piece(j)], raw_mid.at[piece(j)], TO_MID, j, onward)

    def lse_to_mid():
        return copy(text_lse_hbm, lse_mid, TO_MID, PIECES, onward)

    def to_image():
        return copy(image_hbm, raw_image, TO_IMAGE, 0, lower)

    def lse_to_image():
        return copy(image_lse_hbm, lse_image, TO_IMAGE, PIECES, lower)

    def back_far(k):
        return copy(g_far.at[piece(k)], got_far.at[piece(k)], BACK_FAR, k, behind)

    def back_mid(k):
        return copy(g_mid.at[piece(k)], got_mid.at[piece(k)], BACK_MID, k, partner)

    def back_image():
        return copy(g_image.at[pl.ds(rows, rows)], got_image, BACK_IMAGE, 0, higher)

    lse_to_far().start()
    lse_to_mid().start()
    lse_to_image().start()
    for j in range(DIRECT):
        to_mid_direct(j).start()
    for j in range(PIECES):
        to_far(j).start()

        if j >= DIRECT:
            @pl.when(even)
            def _():
                to_mid(j, text_hbm).start()

        if j == 0:
            to_image().start()

    def take_text(which, raw, k):
        unit, _ = unit_rows(raw[part(k), :])
        text_high[which, part(k), :], text_low[which, part(k), :] = split(unit)

    def take_column(which, lse):
        text_column[which] = jnp.transpose(jnp.broadcast_to(lse[...], (128, rows)))

    def take_image(first, raw):
        @pl.loop(0, CHUNKS)
        def _(k):
            unit, _ = unit_rows(raw[part(k), :])
            here = pl.ds(pl.multiple_of(first + k * chunk, chunk), chunk)
            image_high[here, :], image_low[here, :] = split(unit)

    def tile(which, here, columns, lse, diagonal=False):
        text = (text_high[which, here, :], text_low[which, here, :])
        image = (image_high[columns, :], image_low[columns, :])
        scores = logit_scale * dot_split(text, image, NT)
        weight = (0.5 * logit_scale) * (
            jnp.exp(scores - lse) + jnp.exp(scores - text_column[which, here, 0:1])
        )
        if diagonal:
            row = lax.broadcasted_iota(jnp.int32, weight.shape, 0)
            column = lax.broadcasted_iota(jnp.int32, weight.shape, 1)
            weight = weight - jnp.where(row == column, logit_scale, 0.0)
        weights[which, here, columns] = weight
        return dot_split(split(weight), image, NN)

    first, second, both = pl.ds(0, rows), pl.ds(rows, rows), pl.ds(0, 2 * rows)

    def image_grad(half):
        turned = jnp.concatenate([jnp.transpose(weights[which, :, half]) for which in range(3)], axis=1)
        texts = [ref[...].reshape(3 * rows, width) for ref in (text_high, text_low)]
        return dot_split(split(turned), texts, NN)

    load_image.wait()
    take_image(0, image_ref)
    load_text_lse.wait()
    load_image_lse.wait()
    take_column(OWN, text_lse_ref)
    load_text.wait()

    @pl.loop(0, CHUNKS)
    def _(k):
        take_text(OWN, text_ref, k)

    g_own[...] = tile(OWN, first, first, image_lse_ref[...], diagonal=True)

    lse_to_far().wait_recv()

    take_column(FAR, lse_far)

    def receive_far(j):
        @pl.when(odd)
        def _():
            to_far(j).wait_recv()
            if isinstance(j, int) and j < DIRECT:
                return
            to_mid(j, raw_far).start()

    for j in range(PIECES // 2):
        receive_far(j)
    lse_to_image().wait_recv()
    to_image().wait_recv()
    take_image(rows, raw_image)

    g_own[...] += tile(OWN, first, second, lse_image[...])

    lse_to_mid().wait_recv()
    take_column(MID, lse_mid)
    both_lse = jnp.concatenate([image_lse_ref[...], lse_image[...]], axis=1)

    def pass_on(j):
        @pl.when(odd)
        def _():
            back_mid(j).wait_recv()
            g_far[piece(j), :] += got_mid[piece(j), :]
            back_far(j).start()

    half = PIECES // 2
    per = PIECES // CHUNKS

    @pl.loop(0, CHUNKS)
    def _(k):
        late = k >= CHUNKS // 2
        early = k < CHUNKS // 2

        @pl.when(late)
        def _():
            pass_on(2 * k - half)

        for j in range(per):
            to_mid(per * k + j, text_hbm).wait_recv()
        take_text(MID, raw_mid, k)
        g_mid[part(k), :] = tile(MID, part(k), both, both_lse)

        @pl.when(jnp.logical_or(even, late))
        def _():
            for j in range(per):
                back_mid(per * k + j).start()

        @pl.when(early)
        def _():
            receive_far(half + 2 * k)

        @pl.when(late)
        def _():
            pass_on(2 * k + 1 - half)

        @pl.when(even)
        def _():
            for j in range(per):
                to_far(per * k + j).wait_recv()

        take_text(FAR, raw_far, k)
        g_far[part(k), :] = tile(FAR, part(k), both, both_lse)

        @pl.when(even)
        def _():
            for j in range(per):
                back_far(per * k + j).start()

        @pl.when(early)
        def _():
            receive_far(half + 2 * k + 1)

        @pl.when(jnp.logical_and(odd, k == CHUNKS // 2 - 1))
        def _():
            for j in range(half):
                back_mid(j).start()

    pass_on(half)
    g_image[second, :] = image_grad(second)
    back_image().start()
    pass_on(half + 1)
    g_image[first, :] = image_grad(first)
    pass_on(half + 2)
    pass_on(half + 3)
    back_image().wait_recv()

    @pl.loop(0, CHUNKS)
    def _(k):
        grad_image_ref[part(k), :] = project_back(
            g_image[part(k), :] + got_image[part(k), :], image_ref[part(k), :]
        )
        store_image(k).start()

    @pl.loop(0, CHUNKS)
    def _(k):
        @pl.when(even)
        def _():
            for j in range(per):
                back_mid(per * k + j).wait_recv()
            g_own[part(k), :] += got_mid[part(k), :]

        for j in range(per):
            back_far(per * k + j).wait_recv()
        grad_text_ref[part(k), :] = project_back(
            g_own[part(k), :] + got_far[part(k), :], text_ref[part(k), :]
        )
        store_text(k).start()

    lse_to_far().wait_send()
    lse_to_mid().wait_send()
    lse_to_image().wait_send()
    to_image().wait_send()
    back_image().wait_send()

    @pl.loop(0, PIECES)
    def _(k):
        to_far(k).wait_send()
        to_mid(k, text_hbm).wait_send()
        back_far(k).wait_send()
        back_mid(k).wait_send()

    @pl.loop(0, CHUNKS)
    def _(k):
        store_image(k).wait()
        store_text(k).wait()


def solution(mesh):
    n_blk, n_group = mesh.shape["blk"], mesh.shape["group"]

    def per_device(image_embed, text_embed, image_lse, text_lse):
        rows, width = image_embed.shape
        block = jax.ShapeDtypeStruct((rows, width), jnp.float32)
        whole = pltpu.VMEM((rows, width), jnp.float32)
        line = pltpu.VMEM((1, rows), jnp.float32)
        grads = pl.pallas_call(
            functools.partial(kernel, n_blk, n_group),
            out_shape=(block, block),
            in_specs=[pl.BlockSpec(memory_space=pl.ANY)] * 4,
            out_specs=[pl.BlockSpec(memory_space=pl.ANY)] * 2,
            scratch_shapes=[
                whole, whole, line, line, pltpu.SemaphoreType.DMA((4,)),
                whole, whole, pltpu.SemaphoreType.DMA((2, CHUNKS)),
                whole, whole, whole, line, line, line,
                pltpu.VMEM((3, rows, width), jnp.bfloat16),
                pltpu.VMEM((3, rows, width), jnp.bfloat16),
                pltpu.VMEM((3, rows, 128), jnp.float32),
                pltpu.VMEM((2 * rows, width), jnp.bfloat16),
                pltpu.VMEM((2 * rows, width), jnp.bfloat16),
                pltpu.VMEM((3, rows, 2 * rows), jnp.float32),
                whole, whole, whole, whole, whole,
                pltpu.VMEM((2 * rows, width), jnp.float32),
                whole,
                pltpu.SemaphoreType.DMA((6, PIECES + 1)),
                pltpu.SemaphoreType.DMA((6, PIECES + 1)),
            ],
            compiler_params=pltpu.CompilerParams(
                collective_id=0, has_side_effects=True, vmem_limit_bytes=62 * 1024 * 1024
            ),
        )(image_embed, text_embed, image_lse.reshape(1, rows), text_lse.reshape(1, rows))
        return grads

    spec = P(("blk", "group"), None)
    line = P(("blk", "group"))
    return jax.shard_map(
        per_device, mesh=mesh, in_specs=(spec, spec, line, line), out_specs=(spec, spec), check_vma=False
    )
```

time: 57.4 us -> 53.3 us (0.929)
  Pallas kernels: 51.3 us -> 49.5 us
  local copies, waits for them, and re-layouts: 4.71 us -> 3.02 us
    pallas_call x1, Pallas kernels: 51.3 us -> 49.5 us  [per_device(): pl.pallas_call(functools.partial(kernel, n_blk, n_group), out_shape=(bloc...]
    unnamed x10 -> x4, local copies, waits for them, and re-layouts: 4.71 us -> 3.02 us
where the time goes in v2:
time: 53.3 us; the launch traced here: 53.2 us
  Pallas kernels  49.5 us (93%)
  local copies, waits for them, and re-layouts  3.02 us (6%)
  between operations  0.65 us (1%)
    pallas_call x1, Pallas kernels, per_device(): pl.pallas_call(functools.partial(kernel, n_blk, n_group), out_shape=(bloc...  49.5 us
    unnamed x4, local copies, waits for them, and re-layouts  3.02 us

profile of v2, /device:TPU:0, one launch (start us, length us, event | category | flops | bytes accessed | tf_op | source)
XLA Modules:
  0.0 53.2 jit_solution(16704520213293715861)
XLA Ops:
  0.6 49.5 %shard_map.59 = (f32[256,768]{1,0:T(8,128)}, f32[256,768]{1,0:T(8,128)}) custom-call(f32[256,768]{1,0:T(8,128)} %image_hbm.1, f32[256,768]{1,0:T(8,128)} %text_hbm.1, f32[1,256]{1,0:T(1,128)} %bitcast.2, f32[1,256]{1,0:T(1,128)} %bitcast.3), custom_call_target="tpu_custom_call" | custom-call | tf_op jit(solution)/shard_map/pallas_call | solution.py:334
  50.1 0.0 copy-start
  50.1 2.1 %copy.8 = f32[256,768]{1,0:T(8,128)} copy(f32[256,768]{1,0:T(8,128)} %get-tuple-element.4) | data formatting | bytes 1572864
  52.3 0.0 copy-done
  52.3 0.9 %copy.9 = f32[256,768]{1,0:T(8,128)} copy(f32[256,768]{1,0:T(8,128)S(1)} %copy-done) | data formatting | bytes 1572864
Async XLA Ops:
  50.1 2.1 %copy-start = (f32[256,768]{1,0:T(8,128)S(1)}, f32[256,768]{1,0:T(8,128)}, u32[]{:S(2)}) copy-start(f32[256,768]{1,0:T(8,128)} %get-tuple-element.5) | copy-start | bytes 2359300

commit v3 on v2

--- a/solution.py
+++ b/solution.py
@@ -44,9 +44,8 @@
 
 def kernel(
     n_blk, n_group,
-    image_hbm, text_hbm, image_lse_hbm, text_lse_hbm, grad_image_hbm, grad_text_hbm,
+    image_hbm, text_hbm, image_lse_hbm, text_lse_hbm, grad_image_ref, grad_text_ref,
     image_ref, text_ref, image_lse_ref, text_lse_ref, load_sem,
-    grad_image_ref, grad_text_ref, store_sem,
     raw_far, raw_mid, raw_image, lse_far, lse_mid, lse_image,
     text_high, text_low, text_column, image_high, image_low, weights,
     g_own, g_far, g_mid, got_far, got_mid, g_image, got_image,
@@ -96,12 +95,6 @@
     def to_mid(k, source):
         return copy(source.at[piece(k)], raw_mid.at[piece(k)], TO_MID, k, partner)
 
-    def store_image(k):
-        return pltpu.make_async_copy(grad_image_ref.at[part(k)], grad_image_hbm.at[part(k)], store_sem.at[0, k])
-
-    def store_text(k):
-        return pltpu.make_async_copy(grad_text_ref.at[part(k)], grad_text_hbm.at[part(k)], store_sem.at[1, k])
-
     def lse_to_far():
         return copy(text_lse_hbm, lse_far, TO_FAR, PIECES, ahead)
 
@@ -287,7 +280,6 @@
         grad_image_ref[part(k), :] = project_back(
             g_image[part(k), :] + got_image[part(k), :], image_ref[part(k), :]
         )
-        store_image(k).start()
 
     @pl.loop(0, CHUNKS)
     def _(k):
@@ -302,7 +294,6 @@
         grad_text_ref[part(k), :] = project_back(
             g_own[part(k), :] + got_far[part(k), :], text_ref[part(k), :]
         )
-        store_text(k).start()
 
     lse_to_far().wait_send()
     lse_to_mid().wait_send()
@@ -316,11 +307,6 @@
         to_mid(k, text_hbm).wait_send()
         back_far(k).wait_send()
         back_mid(k).wait_send()
-
-    @pl.loop(0, CHUNKS)
-    def _(k):
-        store_image(k).wait()
-        store_text(k).wait()
 
 
 def solution(mesh):
@@ -333,12 +319,11 @@
         line = pltpu.VMEM((1, rows), jnp.float32)
         grads = pl.pallas_call(
             functools.partial(kernel, n_blk, n_group),
-            out_shape=(block, block),
+            out_shape=(whole, whole),
             in_specs=[pl.BlockSpec(memory_space=pl.ANY)] * 4,
-            out_specs=[pl.BlockSpec(memory_space=pl.ANY)] * 2,
+            out_specs=[pl.BlockSpec(memory_space=pltpu.VMEM)] * 2,
             scratch_shapes=[
                 whole, whole, line, line, pltpu.SemaphoreType.DMA((4,)),
-                whole, whole, pltpu.SemaphoreType.DMA((2, CHUNKS)),
                 whole, whole, whole, line, line, line,
                 pltpu.VMEM((3, rows, width), jnp.bfloat16),
                 pltpu.VMEM((3, rows, width), jnp.bfloat16),

time: 53.3 us -> 51.4 us (0.964)
  local copies, waits for them, and re-layouts: 3.02 us -> 1.76 us
  Pallas kernels: 49.5 us -> 48.8 us
    unnamed x4 -> x2, local copies, waits for them, and re-layouts: 3.02 us -> 1.76 us
    pallas_call x1, Pallas kernels: 49.5 us -> 48.8 us  [per_device(): pl.pallas_call(functools.partial(kernel, n_blk, n_group), out_shape=(whol...]
where the time goes in v3:
time: 51.4 us; the launch traced here: 51.2 us
  Pallas kernels  48.8 us (95%)
  local copies, waits for them, and re-layouts  1.76 us (3%)
  between operations  0.64 us (1%)
    pallas_call x1, Pallas kernels, per_device(): pl.pallas_call(functools.partial(kernel, n_blk, n_group), out_shape=(whol...  48.8 us
    unnamed x2, local copies, waits for them, and re-layouts  1.76 us

profile of v3, /device:TPU:0, one launch (start us, length us, event | category | flops | bytes accessed | tf_op | source)
XLA Modules:
  0.0 51.2 jit_solution(830122518700521411)
XLA Ops:
  0.6 48.8 %shard_map.59 = (f32[256,768]{1,0:T(8,128)S(1)}, f32[256,768]{1,0:T(8,128)S(1)}) custom-call(f32[256,768]{1,0:T(8,128)} %image_hbm.1, f32[256,768]{1,0:T(8,128)} %text_hbm.1, f32[1,256]{1,0:T(1,128)} %bitcast.2, f32[1,256]{1,0:T(1,128)} %bitcast.3), custom_call_target="tpu_custom_call" | custom-call | tf_op jit(solution)/shard_map/pallas_call | solution.py:320
  49.5 0.9 %copy.8 = f32[256,768]{1,0:T(8,128)} copy(f32[256,768]{1,0:T(8,128)S(1)} %get-tuple-element.2) | data formatting | bytes 1572864
  50.3 0.9 %copy.9 = f32[256,768]{1,0:T(8,128)} copy(f32[256,768]{1,0:T(8,128)S(1)} %get-tuple-element.3) | data formatting | bytes 1572864

commit v4 on v3

--- a/solution.py
+++ b/solution.py
@@ -195,13 +195,15 @@
                 return
             to_mid(j, raw_far).start()
 
-    for j in range(PIECES // 2):
+    for j in range(PIECES // 2 - 1):
         receive_far(j)
     lse_to_image().wait_recv()
     to_image().wait_recv()
     take_image(rows, raw_image)
 
+    receive_far(PIECES // 2 - 1)
     g_own[...] += tile(OWN, first, second, lse_image[...])
+    receive_far(PIECES // 2)
 
     lse_to_mid().wait_recv()
     take_column(MID, lse_mid)
@@ -215,6 +217,12 @@
             back_far(j).start()
 
     half = PIECES // 2
+
+    def receive_last(j):
+        @pl.when(j < PIECES)
+        def _():
+            receive_far(j)
+
     per = PIECES // CHUNKS
 
     @pl.loop(0, CHUNKS)
@@ -238,7 +246,7 @@
 
         @pl.when(early)
         def _():
-            receive_far(half + 2 * k)
+            receive_far(half + 1 + 2 * k)
 
         @pl.when(late)
         def _():
@@ -259,7 +267,7 @@
 
         @pl.when(early)
         def _():
-            receive_far(half + 2 * k + 1)
+            receive_last(half + 2 + 2 * k)
 
         @pl.when(jnp.logical_and(odd, k == CHUNKS // 2 - 1))
         def _():

time: 51.4 us -> 50.6 us (0.984)
  Pallas kernels: 48.8 us -> 48 us
    pallas_call x1, Pallas kernels: 48.8 us -> 48 us  [per_device(): pl.pallas_call(functools.partial(kernel, n_blk, n_group), out_shape=(whol...]
where the time goes in v4:
time: 50.6 us; the launch traced here: 50.4 us
  Pallas kernels  48 us (95%)
  local copies, waits for them, and re-layouts  1.76 us (3%)
  between operations  0.64 us (1%)
    pallas_call x1, Pallas kernels, per_device(): pl.pallas_call(functools.partial(kernel, n_blk, n_group), out_shape=(whol...  48 us
    unnamed x2, local copies, waits for them, and re-layouts  1.76 us

profile of v4, /device:TPU:0, one launch (start us, length us, event | category | flops | bytes accessed | tf_op | source)
XLA Modules:
  0.0 50.4 jit_solution(1249274549685927515)
XLA Ops:
  0.6 48.0 %shard_map.59 = (f32[256,768]{1,0:T(8,128)S(1)}, f32[256,768]{1,0:T(8,128)S(1)}) custom-call(f32[256,768]{1,0:T(8,128)} %image_hbm.1, f32[256,768]{1,0:T(8,128)} %text_hbm.1, f32[1,256]{1,0:T(1,128)} %bitcast.2, f32[1,256]{1,0:T(1,128)} %bitcast.3), custom_call_target="tpu_custom_call" | custom-call | tf_op jit(solution)/shard_map/pallas_call | solution.py:328
  48.7 0.9 %copy.8 = f32[256,768]{1,0:T(8,128)} copy(f32[256,768]{1,0:T(8,128)S(1)} %get-tuple-element.2) | data formatting | bytes 1572864
  49.6 0.9 %copy.9 = f32[256,768]{1,0:T(8,128)} copy(f32[256,768]{1,0:T(8,128)S(1)} %get-tuple-element.3) | data formatting | bytes 1572864

commit v5 on v4

--- a/solution.py
+++ b/solution.py
@@ -119,9 +119,6 @@
     def back_image():
         return copy(g_image.at[pl.ds(rows, rows)], got_image, BACK_IMAGE, 0, higher)
 
-    lse_to_far().start()
-    lse_to_mid().start()
-    lse_to_image().start()
     for j in range(DIRECT):
         to_mid_direct(j).start()
     for j in range(PIECES):
@@ -134,6 +131,9 @@
 
         if j == 0:
             to_image().start()
+            lse_to_far().start()
+            lse_to_mid().start()
+            lse_to_image().start()
 
     def take_text(which, raw, k):
         unit, _ = unit_rows(raw[part(k), :])
@@ -202,7 +202,6 @@
     take_image(rows, raw_image)
 
     receive_far(PIECES // 2 - 1)
-    g_own[...] += tile(OWN, first, second, lse_image[...])
     receive_far(PIECES // 2)
 
     lse_to_mid().wait_recv()
@@ -273,6 +272,8 @@
         def _():
             for j in range(half):
                 back_mid(j).start()
+
+    g_own[...] += tile(OWN, first, second, lse_image[...])
 
     pass_on(half)
     g_image[second, :] = image_grad(second)

time: 50.6 us -> 50.6 us (level)
  no operation moved by 1% of the time
where the time goes in v5:
time: 50.6 us; the launch traced here: 50.4 us
  Pallas kernels  48 us (95%)
  local copies, waits for them, and re-layouts  1.76 us (3%)
  between operations  0.64 us (1%)
    pallas_call x1, Pallas kernels, per_device(): pl.pallas_call(functools.partial(kernel, n_blk, n_group), out_shape=(whol...  48 us
    unnamed x2, local copies, waits for them, and re-layouts  1.76 us

profile of v5, /device:TPU:0, one launch (start us, length us, event | category | flops | bytes accessed | tf_op | source)
XLA Modules:
  0.0 50.4 jit_solution(12272705221891251100)
XLA Ops:
  0.6 48.0 %shard_map.59 = (f32[256,768]{1,0:T(8,128)S(1)}, f32[256,768]{1,0:T(8,128)S(1)}) custom-call(f32[256,768]{1,0:T(8,128)} %image_hbm.1, f32[256,768]{1,0:T(8,128)} %text_hbm.1, f32[1,256]{1,0:T(1,128)} %bitcast.2, f32[1,256]{1,0:T(1,128)} %bitcast.3), custom_call_target="tpu_custom_call" | custom-call | tf_op jit(solution)/shard_map/pallas_call | solution.py:329
  48.7 0.9 %copy.8 = f32[256,768]{1,0:T(8,128)} copy(f32[256,768]{1,0:T(8,128)S(1)} %get-tuple-element.2) | data formatting | bytes 1572864
  49.5 0.9 %copy.9 = f32[256,768]{1,0:T(8,128)} copy(f32[256,768]{1,0:T(8,128)S(1)} %get-tuple-element.3) | data formatting | bytes 1572864
